TPU v7x, 128 devices: a whole 4x4x4 slice. The times are simulated.
128 devices in a mesh: band: 8 (over x_hi, y), dom: 16 (over x_lo, z, core).
Axes of the slice: x: 4 (x_hi: 2, x_lo: 2; x = x_hi * 2 + x_lo), y: 4, z: 4, core: 2. Of those that a mesh axis runs over, the one named last changes fastest.
Arguments:
- orbitals: bfloat16 [192, 128, 3200], P('band', None, 'dom'), may hold values from -6 to 6
- rotation: bfloat16 [192, 192], P('band'), may hold values from -0.4375 to 0.4375
- potential: float32 [128, 3200], P('dom'), may hold values from -1.5 to 0.5
Outputs:
- filtered: float32 [192, 128, 3200], P('band', 'dom')
All inputs are finite; a program needn't handle non-finite values.
Results may differ from a plain program's by a relative error of at most 0.0029.
Values may be sent and summed in bfloat16 or wider, within the bound.
A program may use at most 256 MiB of HBM per device.

v0:
```python
import jax
import jax.numpy as jnp
from jax import lax
from jax.sharding import PartitionSpec as P

NY = 80
PASSES = 4


potential_offset = 0.5
near_weight = 2.0 / 3.0
far_weight = 1.0 / 24.0
half_range = 4.25


def extended_2(cells, sides, width):
    for axis, dim in sides:
        count = lax.axis_size(axis)
        ends = count - 1
        head = lax.slice_in_dim(cells, 0, width, axis=dim)
        tail = lax.slice_in_dim(cells, cells.shape[dim] - width, cells.shape[dim], axis=dim)
        cells = jnp.concatenate(
            [
                lax.ppermute(tail, axis, [(i, (i + 1) % count) for i in range(ends)]),
                cells,
                lax.ppermute(head, axis, [((i + 1) % count, i) for i in range(ends)]),
            ],
            axis=dim,
        )
    return cells


def shift_columns(values, offset):
    column_y = jnp.arange(values.shape[-1]) % NY
    source = column_y - offset
    inside = (source >= 0) & (source < NY)
    wrapped = offset - NY if offset > 0 else offset + NY
    return jnp.where(inside, jnp.roll(values, offset, -1), jnp.roll(values, wrapped, -1))


def shifted_operator(extended, potential_rows):
    center = extended[:, 2:-2]
    nearest = extended[:, 1:-3] + extended[:, 3:-1]
    nearest = nearest + jnp.roll(center, NY, -1) + jnp.roll(center, -NY, -1)
    nearest = nearest + shift_columns(center, 1) + shift_columns(center, -1)
    second = extended[:, :-4] + extended[:, 4:]
    second = second + jnp.roll(center, 2 * NY, -1) + jnp.roll(center, -2 * NY, -1)
    second = second + shift_columns(center, 2) + shift_columns(center, -2)
    return (
        (potential_rows - potential_offset) * center - near_weight * nearest + far_weight * second
    )


def body(orbitals, rotation, potential):
    gathered = lax.all_to_all(orbitals, "band", split_axis=1, concat_axis=0, tiled=True)
    full_matrix = lax.all_gather(rotation, "band", axis=0, tiled=True)
    flattened = gathered.reshape(gathered.shape[0], gathered.shape[1] * gathered.shape[2])
    rotated = lax.dot_general(
        full_matrix, flattened, (((0,), (0,)), ((), ())), preferred_element_type=jnp.float32
    )
    rotated = rotated.astype(jnp.bfloat16).reshape(gathered.shape)
    domains = lax.all_to_all(
        lax.all_to_all(rotated, "band", split_axis=0, concat_axis=1, tiled=True),
        "dom",
        split_axis=1,
        concat_axis=2,
        tiled=True,
    )
    start_field = domains.astype(jnp.float32)
    previous = start_field
    current = start_field
    for order in range(PASSES):
        extended = extended_2(current, (("dom", 1),), 2)
        operated = shifted_operator(extended, potential)
        if order == 0:
            following = operated / half_range
        else:
            following = 2.0 / half_range * operated - previous
        previous, current = (current, following)
    return current


def solution(mesh):
    in_specs = (P("band", None, "dom"), P("band", None), P("dom", None))
    out_specs = P("band", "dom", None)
    return jax.shard_map(body, mesh=mesh, in_specs=in_specs, out_specs=out_specs, check_vma=False)
```

profile of v0, /device:TPU:97, one launch (start us, length us, event | category | flops | bytes accessed | tf_op | source)
XLA Modules:
  0.0 256.5 jit_solution(4761323935283309326)
XLA Ops:
  0.0 2.8 %copy.10 = bf16[24,128,200]{2,0,1:T(8,128)(2,1)} copy(bf16[24,128,200]{1,2,0:T(8,128)(2,1)} %param.3) | data formatting | bytes 2457600 | tf_op args[0]
  2.8 6.7 %all-to-all-start = ((bf16[24,128,200]{2,0,1:T(8,128)(2,1)}), bf16[24,128,200]{2,0,1:T(8,128)(2,1)S(1)}, u32[]{:S(2)}, u32[]{:S(2)}) async-start(bf16[24,128,200]{2,0,1:T(8,128)(2,1)} %copy.10), calls=%async_computation | async-start | bytes 3145728 | tf_op jit(solution)/shard_map/all_to_all | solution.py:55
  9.4 42.8 %all_gather.3 = bf16[192,192]{1,0:T(8,128)(2,1)S(1)} all-gather(bf16[24,192]{1,0:T(8,128)(2,1)S(1)} %copy-done.3), channel_id=1, replica_groups=mesh['band'=8,'dom'=16] {'band'}, dimensions={0}, use_global_device_ids=true | all-gather | bytes 82944 | tf_op jit(solution)/shard_map/all_gather | solution.py:56
  55.5 4.7 %reshape.13 = bf16[192,16,200]{2,1,0:T(8,128)(2,1)S(1)} reshape(bf16[192,3200]{1,0:T(8,128)(2,1)S(1)} %convolution_convert_fusion) | data formatting | bytes 2457600 | tf_op jit(solution)/shard_map/reshape | solution.py:61
  60.2 17.1 %all_to_all.42 = bf16[192,16,200]{2,1,0:T(8,128)(2,1)S(1)} all-to-all(bf16[192,16,200]{2,1,0:T(8,128)(2,1)S(1)} %reshape.13), channel_id=1, replica_groups=mesh['band'=8,'dom'=16] {'band'}, dimensions={0} | all-to-all | bytes 2457600 | tf_op jit(solution)/shard_map/all_to_all | solution.py:63
  79.6 14.3 %all-to-all-start.2 = ((bf16[24,128,200]{2,0,1:T(8,128)(2,1)}), bf16[24,128,200]{2,0,1:T(8,128)(2,1)S(1)}, u32[]{:S(2)}, u32[]{:S(2)}) async-start(bf16[24,128,200]{2,0,1:T(8,128)(2,1)} %copy.14), calls=%async_computation.2 | async-start | bytes 3145728 | tf_op jit(solution)/shard_map/all_to_all | solution.py:62
  94.0 21.9 %all-to-all-done.2 = bf16[24,128,200]{2,0,1:T(8,128)(2,1)S(1)} async-done(((bf16[24,128,200]{2,0,1:T(8,128)(2,1)}), bf16[24,128,200]{2,0,1:T(8,128)(2,1)S(1)}, u32[]{:S(2)}, u32[]{:S(2)}) %all-to-all-start.2) | async-done | bytes 1228832 | tf_op jit(solution)/shard_map/all_to_all | solution.py:62
  116.3 2.8 %copy.16 = f32[24,8,16,200]{3,2,1,0:T(8,128)} copy(f32[24,8,16,200]{3,1,2,0:T(8,128)S(1)} %convert_bitcast_fusion) | data formatting | bytes 4915200 | tf_op jit(solution)/shard_map/convert_element_type | solution.py:69
  119.1 3.5 %reshape.14 = f32[24,8,3200]{2,1,0:T(8,128)S(1)} reshape(f32[24,8,16,200]{3,2,1,0:T(8,128)} %copy.16) | data formatting | bytes 4915200 | tf_op jit(solution)/shard_map/convert_element_type | solution.py:69
  123.3 3.0 %fusion.135 = (f32[24,8,3040]{2,1,0:T(8,128)}, f32[24,8,3040]{2,1,0:T(8,128)}) fusion(f32[24,8,3200]{2,1,0:T(8,128)S(1)} %reshape.14), kind=kLoop, calls=%fused_computation.181 | loop fusion | bytes 9338880 | tf_op jit(solution)/shard_map/jit(_roll_static)/slice | solution.py:47
  131.1 3.0 %fusion.137 = (f32[24,8,3198]{2,1,0:T(8,128)}, f32[24,8,3198]{2,1,0:T(8,128)}) fusion(f32[24,8,3200]{2,1,0:T(8,128)S(1)} %reshape.14), kind=kLoop, calls=%fused_computation.183 | loop fusion | bytes 9824256 | tf_op jit(solution)/shard_map/jit(_roll_static)/slice | solution.py:38
  136.3 2.7 %collective-permute-start.1 = (f32[24,2,3200]{2,1,0:T(2,128)S(1)}, f32[24,2,3200]{2,1,0:T(2,128)S(1)}, u32[]{:S(2)}, u32[]{:S(2)}) collective-permute-start(f32[24,2,3200]{2,1,0:T(2,128)S(1)} %get-tuple-element.98), channel_id=1, source_target_pairs={{1,0},{2,1},{3,2},{4,3},{5,4},{6,5},{7,6},{8,7},{9,8},{10,9},{11,1... | collective-permute-start | bytes 1843208 | tf_op jit(solution)/shard_map/ppermute | solution.py:26
  140.5 9.4 %collective-permute-done.1 = f32[24,2,3200]{2,1,0:T(2,128)S(1)} collective-permute-done((f32[24,2,3200]{2,1,0:T(2,128)S(1)}, f32[24,2,3200]{2,1,0:T(2,128)S(1)}, u32[]{:S(2)}, u32[]{:S(2)}) %collective-permute-start.1) | collective-permute-done | bytes 614432 | tf_op jit(solution)/shard_map/ppermute | solution.py:26
  150.9 10.1 %broadcast_multiply_fusion = (f32[24,8,3200]{2,1,0:T(8,128)S(1)}, f32[24,8,3200]{2,1,0:T(8,128)S(1)}) fusion(f32[24,8,3122]{2,1,0:T(8,128)S(1)} %get-tuple-element.108, f32[24,8,78]{2,1,0:T(8,128)S(1)} %get-tuple-element.110, f32[24,8,2]{2,1,0:T(8,128)S(1)} %get-tuple-element.104, f32[24,8,3198]{2,1,0:T(8,128)} %get-tuple-element.106, ...), kind=kLoop, calls=%fused_computation.108 | loop fusion | flops 20889600 | bytes 42508800 | tf_op jit(solution)/shard_map/div | solution.py:76
  165.2 3.0 %fusion.115 = (f32[24,8,3122]{2,1,0:T(8,128)}, f32[24,8,3122]{2,1,0:T(8,128)}) fusion(f32[24,8,3200]{2,1,0:T(8,128)S(1)} %get-tuple-element.5), kind=kLoop, calls=%fused_computation.161 | loop fusion | bytes 9590784 | tf_op jit(solution)/shard_map/jit(_roll_static)/slice | solution.py:38
  172.7 2.9 %fusion.118 = (f32[24,8,3040]{2,1,0:T(8,128)}, f32[24,8,3040]{2,1,0:T(8,128)}) fusion(f32[24,8,3200]{2,1,0:T(8,128)S(1)} %get-tuple-element.5), kind=kLoop, calls=%fused_computation.164 | loop fusion | bytes 9338880 | tf_op jit(solution)/shard_map/jit(_roll_static)/slice | solution.py:47
  177.2 6.5 %collective-permute-done.3 = f32[24,2,3200]{2,1,0:T(2,128)S(1)} collective-permute-done((f32[24,2,3200]{2,1,0:T(2,128)S(1)}, f32[24,2,3200]{2,1,0:T(2,128)S(1)}, u32[]{:S(2)}, u32[]{:S(2)}) %collective-permute-start.3) | collective-permute-done | bytes 614432 | tf_op jit(solution)/shard_map/ppermute | solution.py:26
  183.7 9.1 %fusion.34 = f32[24,8,3200]{2,1,0:T(8,128)S(1)} fusion(f32[24,8,3200]{2,1,0:T(8,128)S(1)} %reshape.14, f32[24,8,3200]{2,1,0:T(8,128)S(1)} %get-tuple-element.5, f32[24,2,3200]{2,1,0:T(2,128)S(1)} %collective-permute-done.3, f32[24,2,3200]{2,1,0:T(2,128)S(1)} %collective-permute-done.2, f32[24,8,3120]{2,1,0:T(8,128)S(1)} %get-tuple-element.80, ...), kind=kLoop, calls=%fused_computation.50 | loop fusion | flops 22732800 | bytes 40665600 | tf_op jit(solution)/shard_map/sub | solution.py:78
  201.5 2.6 %collective-permute-start.5 = (f32[24,2,3200]{2,1,0:T(2,128)S(1)}, f32[24,2,3200]{2,1,0:T(2,128)S(1)}, u32[]{:S(2)}, u32[]{:S(2)}) collective-permute-start(f32[24,2,3200]{2,1,0:T(2,128)S(1)} %get-tuple-element.58), channel_id=1, source_target_pairs={{1,0},{2,1},{3,2},{4,3},{5,4},{6,5},{7,6},{8,7},{9,8},{10,9},{11,1... | collective-permute-start | bytes 1843208 | tf_op jit(solution)/shard_map/ppermute | solution.py:26
  204.1 3.0 %fusion.105 = (f32[24,8,3040]{2,1,0:T(8,128)}, f32[24,8,3040]{2,1,0:T(8,128)}) fusion(f32[24,8,3200]{2,1,0:T(8,128)S(1)} %fusion.34), kind=kLoop, calls=%fused_computation.151 | loop fusion | bytes 9338880 | tf_op jit(solution)/shard_map/jit(_roll_static)/slice | solution.py:47
  208.6 6.5 %collective-permute-done.5 = f32[24,2,3200]{2,1,0:T(2,128)S(1)} collective-permute-done((f32[24,2,3200]{2,1,0:T(2,128)S(1)}, f32[24,2,3200]{2,1,0:T(2,128)S(1)}, u32[]{:S(2)}, u32[]{:S(2)}) %collective-permute-start.5) | collective-permute-done | bytes 614432 | tf_op jit(solution)/shard_map/ppermute | solution.py:26
  215.9 9.1 %fusion.22 = f32[24,8,3200]{2,1,0:T(8,128)S(1)} fusion(f32[24,8,3200]{2,1,0:T(8,128)S(1)} %fusion.34, f32[24,2,3200]{2,1,0:T(2,128)} %copy-done, f32[24,2,3200]{2,1,0:T(2,128)S(1)} %collective-permute-done.4, f32[24,8,3120]{2,1,0:T(8,128)S(1)} %get-tuple-element.54, f32[24,8,80]{2,1,0:T(8,128)} %get-tuple-element.56, f32[24,8,80]{2,1,0:T(8,128)} %get-tuple-element.55, ...), kind=kLoop, calls=%fused_computation.38 | loop fusion | flops 23347200 | bytes 38208000 | tf_op jit(solution)/shard_map/sub | solution.py:78
  240.2 6.6 %collective-permute-done.7 = f32[24,2,3200]{2,1,0:T(2,128)} collective-permute-done((f32[24,2,3200]{2,1,0:T(2,128)S(1)}, f32[24,2,3200]{2,1,0:T(2,128)}, u32[]{:S(2)}, u32[]{:S(2)}) %collective-permute-start.7) | collective-permute-done | bytes 614432 | tf_op jit(solution)/shard_map/ppermute | solution.py:26
  246.8 9.5 %fusion.10 = f32[24,8,3200]{2,1,0:T(8,128)} fusion(f32[24,8,3200]{2,1,0:T(8,128)S(1)} %fusion.34, f32[24,8,3200]{2,1,0:T(8,128)S(1)} %fusion.22, f32[24,2,3200]{2,1,0:T(2,128)} %collective-permute-done.7, f32[24,2,3200]{2,1,0:T(2,128)S(1)} %collective-permute-done.6, f32[24,8,3120]{2,1,0:T(8,128)S(1)} %get-tuple-element.28, ...), kind=kLoop, calls=%fused_computation.26 | loop fusion | flops 22732800 | bytes 38208000 | tf_op jit(solution)/shard_map/sub | solution.py:78
  (77 shorter events, 52.1 us)
Async XLA Ops:
  0.0 9.4 %copy-start.3 = (bf16[24,192]{1,0:T(8,128)(2,1)S(1)}, bf16[24,192]{1,0:T(8,128)(2,1)}, u32[]{:S(2)}) copy-start(bf16[24,192]{1,0:T(8,128)(2,1)} %param.4) | copy-start | bytes 27652
  2.8 49.5 %all-to-all-start = ((bf16[24,128,200]{2,0,1:T(8,128)(2,1)}), bf16[24,128,200]{2,0,1:T(8,128)(2,1)S(1)}, u32[]{:S(2)}, u32[]{:S(2)}) async-start(bf16[24,128,200]{2,0,1:T(8,128)(2,1)} %copy.10), calls=%async_computation | async-start | bytes 3145728 | tf_op jit(solution)/shard_map/all_to_all | solution.py:55
  77.5 16.4 %copy-start.2 = (f32[8,3200]{1,0:T(8,128)S(1)}, f32[8,3200]{1,0:T(8,128)}, u32[]{:S(2)}) copy-start(f32[8,3200]{1,0:T(8,128)} %param.5) | copy-start | bytes 307204
  79.6 36.3 %all-to-all-start.2 = ((bf16[24,128,200]{2,0,1:T(8,128)(2,1)}), bf16[24,128,200]{2,0,1:T(8,128)(2,1)S(1)}, u32[]{:S(2)}, u32[]{:S(2)}) async-start(bf16[24,128,200]{2,0,1:T(8,128)(2,1)} %copy.14), calls=%async_computation.2 | async-start | bytes 3145728 | tf_op jit(solution)/shard_map/all_to_all | solution.py:62
  134.1 16.0 %collective-permute-start = (f32[24,2,3200]{2,1,0:T(2,128)S(1)}, f32[24,2,3200]{2,1,0:T(2,128)S(1)}, u32[]{:S(2)}, u32[]{:S(2)}) collective-permute-start(f32[24,2,3200]{2,1,0:T(2,128)S(1)} %get-tuple-element.97), channel_id=1, source_target_pairs={{0,1},{1,2},{2,3},{3,4},{4,5},{5,6},{6,7},{7,8},{8,9},{9,10},{10,1... | collective-permute-start | bytes 1843208 | tf_op jit(solution)/shard_map/ppermute | solution.py:24
  136.3 13.6 %collective-permute-start.1 = (f32[24,2,3200]{2,1,0:T(2,128)S(1)}, f32[24,2,3200]{2,1,0:T(2,128)S(1)}, u32[]{:S(2)}, u32[]{:S(2)}) collective-permute-start(f32[24,2,3200]{2,1,0:T(2,128)S(1)} %get-tuple-element.98), channel_id=1, source_target_pairs={{1,0},{2,1},{3,2},{4,3},{5,4},{6,5},{7,6},{8,7},{9,8},{10,9},{11,1... | collective-permute-start | bytes 1843208 | tf_op jit(solution)/shard_map/ppermute | solution.py:26
  150.1 0.8 copy-start.1
  168.2 9.0 %collective-permute-start.2 = (f32[24,2,3200]{2,1,0:T(2,128)S(1)}, f32[24,2,3200]{2,1,0:T(2,128)S(1)}, u32[]{:S(2)}, u32[]{:S(2)}) collective-permute-start(f32[24,2,3200]{2,1,0:T(2,128)S(1)} %get-tuple-element.83), channel_id=1, source_target_pairs={{0,1},{1,2},{2,3},{3,4},{4,5},{5,6},{6,7},{7,8},{8,9},{9,10},{10,1... | collective-permute-start | bytes 1843208 | tf_op jit(solution)/shard_map/ppermute | solution.py:24
  170.1 13.6 %collective-permute-start.3 = (f32[24,2,3200]{2,1,0:T(2,128)S(1)}, f32[24,2,3200]{2,1,0:T(2,128)S(1)}, u32[]{:S(2)}, u32[]{:S(2)}) collective-permute-start(f32[24,2,3200]{2,1,0:T(2,128)S(1)} %get-tuple-element.84), channel_id=1, source_target_pairs={{1,0},{2,1},{3,2},{4,3},{5,4},{6,5},{7,6},{8,7},{9,8},{10,9},{11,1... | collective-permute-start | bytes 1843208 | tf_op jit(solution)/shard_map/ppermute | solution.py:26
  199.6 9.0 %collective-permute-start.4 = (f32[24,2,3200]{2,1,0:T(2,128)S(1)}, f32[24,2,3200]{2,1,0:T(2,128)S(1)}, u32[]{:S(2)}, u32[]{:S(2)}) collective-permute-start(f32[24,2,3200]{2,1,0:T(2,128)S(1)} %get-tuple-element.57), channel_id=1, source_target_pairs={{0,1},{1,2},{2,3},{3,4},{4,5},{5,6},{6,7},{7,8},{8,9},{9,10},{10,1... | collective-permute-start | bytes 1843208 | tf_op jit(solution)/shard_map/ppermute | solution.py:24
  201.5 13.6 %collective-permute-start.5 = (f32[24,2,3200]{2,1,0:T(2,128)S(1)}, f32[24,2,3200]{2,1,0:T(2,128)S(1)}, u32[]{:S(2)}, u32[]{:S(2)}) collective-permute-start(f32[24,2,3200]{2,1,0:T(2,128)S(1)} %get-tuple-element.58), channel_id=1, source_target_pairs={{1,0},{2,1},{3,2},{4,3},{5,4},{6,5},{7,6},{8,7},{9,8},{10,9},{11,1... | collective-permute-start | bytes 1843208 | tf_op jit(solution)/shard_map/ppermute | solution.py:26
  215.1 0.8 copy-start
  231.2 9.0 %collective-permute-start.6 = (f32[24,2,3200]{2,1,0:T(2,128)S(1)}, f32[24,2,3200]{2,1,0:T(2,128)S(1)}, u32[]{:S(2)}, u32[]{:S(2)}) collective-permute-start(f32[24,2,3200]{2,1,0:T(2,128)S(1)} %get-tuple-element.31), channel_id=1, source_target_pairs={{0,1},{1,2},{2,3},{3,4},{4,5},{5,6},{6,7},{7,8},{8,9},{9,10},{10,1... | collective-permute-start | bytes 1843208 | tf_op jit(solution)/shard_map/ppermute | solution.py:24
  233.1 13.7 %collective-permute-start.7 = (f32[24,2,3200]{2,1,0:T(2,128)S(1)}, f32[24,2,3200]{2,1,0:T(2,128)}, u32[]{:S(2)}, u32[]{:S(2)}) collective-permute-start(f32[24,2,3200]{2,1,0:T(2,128)S(1)} %get-tuple-element.32), channel_id=1, source_target_pairs={{1,0},{2,1},{3,2},{4,3},{5,4},{6,5},{7,6},{8,7},{9,8},{10,9},{11,1... | collective-permute-start | bytes 1843208 | tf_op jit(solution)/shard_map/ppermute | solution.py:26
where the time goes:
time: 262 us; the launch traced here: 257 us
  local copies, waits for them, and re-layouts  61.7 us (24%)
  blocking collectives  59.9 us (23%)
  waiting for transfers between devices  56.3 us (21%)
  starting transfers between devices  39.1 us (15%)
  other arithmetic  38.1 us (15%)
    all_gather x1, blocking collectives, body(): full_matrix = lax.all_gather(rotation, 'band', axis=0, tiled=True)  42.8 us
    ppermute x4, waiting for transfers between devices, extended_2(): lax.ppermute(head, axis, [((i + 1) % count, i) for i in range(ends)])  29 us
    sub x3, other arithmetic, body(): following = 2.0 / half_range * operated - previous  27.6 us
    all_to_all x1, waiting for transfers between devices, body(): lax.all_to_all(lax.all_to_all(rotated, 'band', split_axis=0, concat_axis=...  21.9 us
    all_to_all x1, blocking collectives, body(): lax.all_to_all(rotated, 'band', split_axis=0, concat_axis=1, tiled=True)  17.1 us
    all_to_all x1, starting transfers between devices, body(): lax.all_to_all(lax.all_to_all(rotated, 'band', split_axis=0, concat_axis=...  14.3 us
    slice x16, local copies, waits for them, and re-layouts, shift_columns(): jnp.roll(values, offset, -1)  11 us
    slice x16, local copies, waits for them, and re-layouts, shift_columns(): jnp.roll(values, wrapped, -1)  10.5 us
  transfers between devices with their start and end apart: 10, of which 8 were waited for; matrix products, arithmetic and copies ran while one was open for 4% of the time, Pallas kernels for 0%

commit v1 on v0

v1 whole, which is shorter than its diff:
```python
import functools

import jax
import jax.numpy as jnp
import numpy as np
from jax import lax
from jax.experimental import pallas as pl
from jax.experimental.pallas import tpu as pltpu
from jax.sharding import PartitionSpec as P

NY = 80
NXY = 3200
MESH = pl.DeviceIdType.MESH
F32 = jnp.float32
BF16 = jnp.bfloat16

potential_offset = 0.5
near_weight = 2.0 / 3.0
half_range = 4.25

TILES = 13
LANES = 128
SHARE = 200
WIDE = 3328
RING = 256 + WIDE + 256


def target_domain(h, y, z, c, half):
    return lax.rem(h + half, 2) * 8 + lax.rem(z + y + c + 2 * half, 4) * 2 + half


def place():
    band, dom = lax.axis_index("band"), lax.axis_index("dom")
    return band, dom, band // 4, lax.rem(band, 4), dom // 8, lax.rem(dom // 2, 4), lax.rem(dom, 2)


def exchange_kernel(
    orb_ref, rot_ref, pot_ref,
    own_ref, low_ref, high_ref, plow_ref, phigh_ref,
    head, tail, send1, recv1, send2, weights,
    s1, r1, s2, r2, sh, rh, sp, rp, ls,
):
    band, dom, h, y, x, z, c = place()
    mirror = (1 - x) * 8 + z * 2 + c
    has_low, has_high = dom > 0, dom < 15

    def partner(k):
        return lax.rem(h + k // 4, 2), lax.rem(y + lax.rem(k, 4), 4)

    barrier = pltpu.get_barrier_semaphore()

    def greet(b, d):
        pl.semaphore_signal(barrier, inc=1, device_id={"band": b, "dom": d}, device_id_type=MESH)

    for k in range(8):
        hh, yy = partner(k)
        greet(hh * 4 + yy, mirror)
    for half in range(2):
        for k in range(8):
            hh, yy = partner(k)
            greet(hh * 4 + yy, target_domain(h, y, z, c, half))
    for q in range(16):
        qz, qc = (q // 2) % 4, q % 2
        greet(lax.rem(x + c, 2) * 4 + lax.rem(z - qz - qc - 2 * c + 16, 4), q)
    up, down = lax.rem(dom + 1, 16), lax.rem(dom + 15, 16)
    greet(band, up)
    greet(band, down)

    def widen(o, _):
        rows = pl.ds(pl.multiple_of(o * 128, 128), 128)
        v = orb_ref[o].astype(F32)
        head[rows, :] = v[:, :LANES]
        tail[rows, :] = jnp.concatenate([v[:, LANES:], v[:, : 2 * LANES - SHARE]], axis=1)
        return 0

    lax.fori_loop(0, 24, widen, 0)

    lane = lax.broadcasted_iota(jnp.int32, (24, LANES), 1)
    turn = lax.rem(dom * 72, 128)
    r = rot_ref[...].astype(F32)
    r_left = r[:, :LANES]
    r_right = jnp.concatenate([r[:, LANES:], r[:, : 2 * LANES - 192]], axis=1)

    pl.semaphore_wait(barrier, 42)

    pot_copies = []
    for i, (dst, to, ok) in enumerate(((plow_ref, up, has_high), (phigh_ref, down, has_low))):
        cp = pltpu.make_async_remote_copy(
            src_ref=pot_ref, dst_ref=dst, send_sem=sp.at[i], recv_sem=rp.at[i],
            device_id={"band": band, "dom": to}, device_id_type=MESH)
        pot_copies.append(cp)
        pl.when(ok)(cp.start)

    def copy1(slot, source, to):
        return pltpu.make_async_remote_copy(
            src_ref=send1.at[slot], dst_ref=recv1.at[source], send_sem=s1.at[slot], recv_sem=r1.at[source],
            device_id={"band": to, "dom": mirror}, device_id_type=MESH)

    def pack(k, _):
        hh, yy = partner(k)
        parts = []
        for half in range(2):
            first = target_domain(hh, yy, z, c, half) * 8
            tiles = []
            for zz in range(8):
                v = head[pl.ds(first + zz, 24, stride=128), :]
                tiles.append(pltpu.roll(v, turn, 1))
            ends = [tail[pl.ds(first + zz, 24, stride=128), :] for zz in range(8)]
            for zz in range(4):
                v = jnp.where(lane < 64, ends[zz], pltpu.roll(ends[zz + 4], 64, 1))
                tiles.append(pltpu.roll(v, turn, 1))
            v = ends[0]
            for zz in range(1, 8):
                v = jnp.where(lane < 64 + 8 * zz, v, pltpu.roll(ends[zz], 8 * zz, 1))
            tiles.append(pltpu.roll(v, turn, 1))
            parts.append(tiles)
        parts[0].append(r_left)
        parts[1].append(r_right)
        for t in range(TILES + 1):
            a, b = parts[0][t], parts[1][t]
            send1[k, t, 0] = a[:16].astype(BF16)
            send1[k, t, 1] = b[:16].astype(BF16)
            send1[k, t, 2] = jnp.concatenate([a[16:], b[16:]], axis=0).astype(BF16)
        copy1(k, band, hh * 4 + yy).start()
        return 0

    lax.fori_loop(0, 8, pack, 0)
    for k in range(8):
        copy1(k, k, band).wait_recv()

    zero = jnp.zeros((8, 2 * LANES), F32)
    first_rows = jnp.concatenate([
        recv1[:, TILES, 0].astype(F32).reshape(128, LANES),
        recv1[:, TILES, 1].astype(F32).reshape(128, LANES)], axis=1)
    for half in range(2):
        rows = [first_rows]
        for k in range(8):
            m = recv1[k, TILES, 2].astype(F32)
            m = jnp.concatenate([m[:8], m[8:]], axis=1)
            rows += [m, zero] if half == 0 else [zero, m]
        weights[half] = jnp.transpose(jnp.concatenate(rows, axis=0))[:192].astype(BF16)

    lane8 = lax.broadcasted_iota(jnp.int32, (8, LANES), 1)
    in_window = lax.rem(lane8 - lax.rem(mirror * 72, 128) + 64 + 128, 128) < 64

    def copy2(slot, source, b, d):
        return pltpu.make_async_remote_copy(
            src_ref=send2.at[slot], dst_ref=own_ref.at[source], send_sem=s2.at[slot], recv_sem=r2.at[source],
            device_id={"band": b, "dom": d}, device_id_type=MESH)

    self_sent = False
    for half in range(2):
        def rhs(t):
            return jnp.concatenate(
                [recv1[:, t, half].reshape(128, LANES), recv1[:, t, 2].reshape(128, LANES)], axis=0)

        def pair(i, _):
            both = jnp.concatenate([rhs(2 * i), rhs(2 * i + 1)], axis=1)
            out = jnp.dot(weights[half], both, preferred_element_type=F32)
            for b in range(8):
                for g in range(3):
                    v = out[24 * b + 8 * g : 24 * b + 8 * g + 8]
                    v = jnp.concatenate([v[:, :LANES], v[:, LANES:]], axis=0)
                    send2[half * 8 + b, 6 * g + i] = v.astype(BF16)
            return 0

        lax.fori_loop(0, 6, pair, 0)
        out = jnp.dot(weights[half], rhs(12), preferred_element_type=F32)
        for b in range(8):
            v = out[24 * b : 24 * b + 24]
            first = jnp.where(in_window, v[:8], pltpu.roll(v[16:], 64, 1))
            send2[half * 8 + b, 18] = jnp.concatenate([first, v[8:16]], axis=0).astype(BF16)
        to_dom = target_domain(h, y, z, c, half)
        is_self = to_dom == dom
        self_sent = jnp.logical_or(self_sent, is_self)

        def post(k, _):
            hh, yy = partner(k)
            to = hh * 4 + yy
            here = jnp.logical_and(is_self, k == 0)

            @pl.when(jnp.logical_not(here))
            def _():
                copy2(half * 8 + to, mirror, to, to_dom).start()

            @pl.when(here)
            def _():
                pltpu.make_async_copy(send2.at[half * 8 + to], own_ref.at[mirror], ls).start()

            return 0

        lax.fori_loop(0, 8, post, 0)

    for q in range(16):
        here = jnp.logical_and(self_sent, mirror == q)

        @pl.when(jnp.logical_not(here))
        def _():
            copy2(q, q, band, dom).wait_recv()

        @pl.when(here)
        def _():
            pltpu.make_async_copy(send2.at[0], own_ref.at[q], ls).wait()

    halo = []
    for i, (dst, to, ok) in enumerate(((low_ref, up, has_high), (high_ref, down, has_low))):
        cp = pltpu.make_async_remote_copy(
            src_ref=own_ref, dst_ref=dst, send_sem=sh.at[i], recv_sem=rh.at[i],
            device_id={"band": band, "dom": to}, device_id_type=MESH)
        halo.append(cp)
        pl.when(ok)(cp.start)

    for k in range(8):
        copy1(k, k, band).wait_send()
    for half in range(2):
        is_self = target_domain(h, y, z, c, half) == dom
        for b in range(8):
            @pl.when(jnp.logical_not(jnp.logical_and(is_self, band == b)))
            def _():
                copy2(half * 8 + b, 0, band, dom).wait_send()
    for i, ok_send, ok_recv in ((0, has_high, has_low), (1, has_low, has_high)):
        pl.when(ok_send)(pot_copies[i].wait_send)
        pl.when(ok_recv)(pot_copies[i].wait_recv)
        pl.when(ok_send)(halo[i].wait_send)
        pl.when(ok_recv)(halo[i].wait_recv)


def neighbour_weights():
    out = np.zeros((5, 768, 256), np.float32)
    for w in range(5):
        for col in range(256):
            cell = 256 * w + col
            cy = cell % NY
            for step, value in ((1, 1.0), (2, -1.0 / 16.0)):
                for sign in (-1, 1):
                    out[w, col + 256 + sign * step * NY, col] += value
                    out[w, col + 256 + (cy + sign * step) % NY - cy, col] += value
    return out


def filter_kernel(
    own_ref, own_x, low_ref, low_x, high_ref, high_x, pot_ref, plow_ref, phigh_ref, w_ref,
    out_ref,
    even, odd, ring0, ring1, scaled, done,
):
    dom = lax.axis_index("dom")
    g = pl.program_id(0)
    inside = (dom > 0, None, dom < 15)
    lane = lax.broadcasted_iota(jnp.int32, (8, LANES), 1)

    @pl.when(g == 0)
    def _():
        for region, ref in enumerate((plow_ref, pot_ref, phigh_ref)):
            for zz in range(8):
                v = (ref[zz : zz + 1, :] - potential_offset) * (2.0 / half_range)
                if inside[region] is not None:
                    v = jnp.where(inside[region], v, 0.0)
                rows = pl.ds(64 * region + 8 * zz, 8)
                scaled[rows, :NXY] = jnp.broadcast_to(v, (8, NXY))
        scaled[:, NXY:] = jnp.zeros((192, WIDE - NXY), F32)
        even[:, NXY:] = jnp.zeros((192, WIDE - NXY), F32)
        odd[:, NXY:] = jnp.zeros((192, WIDE - NXY), F32)

    for region, (ref, xref) in enumerate(((low_ref, low_x), (own_ref, own_x), (high_ref, high_x))):
        last = []
        for d in range(16):
            v = xref[d, 0].astype(F32)
            v = jnp.where(g == 1, v[8:], v[:8])
            last.append(jnp.where(g == 2, pltpu.roll(v, 64, 1), v))
        for i in range(4):
            eights = []
            for zz in (2 * i, 2 * i + 1):
                v = None
                for d in range(16):
                    unit = (9 * d + 8 + zz) % 16
                    own = (lane // 8) == unit
                    v = last[d] if v is None else jnp.where(own, last[d], v)
                eights.append(pltpu.roll(v, (128 - 8 * zz) % 128, 1) if zz else v)
            pieces = [[] for _ in range(25)]
            for d in range(16):
                o, t0 = SHARE * d % 128, SHARE * d // 128
                hd = ref[d, i].astype(F32)
                pair = ((2 * i) % 4) // 2
                td = ref[d, 4 + pair].astype(F32)
                if i >= 2:
                    td = pltpu.roll(td, 64, 1)
                pieces[t0].append((o, 128, hd))
                if o:
                    pieces[t0 + 1].append((0, o, hd))
                end = o + 64
                pieces[t0 + 1].append((o, min(end, 128), td))
                if end > 128:
                    pieces[t0 + 2].append((0, end - 128, td))
                e = SHARE * d + 192
                pieces[e // 128].append((e % 128, e % 128 + 8, None))
            for t in range(25):
                ps = sorted(pieces[t], key=lambda p: p[0])
                assert ps[0][0] == 0 and ps[-1][1] == 128
                both = []
                for j in range(2):
                    v = None
                    for lo, hi, src in ps:
                        s = eights[j] if src is None else src[8 * j : 8 * j + 8]
                        v = s if v is None else jnp.where(lane < lo, v, s)
                    if inside[region] is not None:
                        v = jnp.where(inside[region], v, 0.0)
                    both.append(v)
                rows = slice(64 * region + 16 * i, 64 * region + 16 * i + 16)
                v = jnp.concatenate(both, axis=0)
                even[rows, 128 * t : 128 * t + 128] = v
                ring0[rows, 256 + 128 * t : 384 + 128 * t] = v.astype(BF16)

    def close(ring, first, last):
        rows = slice(8 * first, 8 * last)
        ring[rows, :256] = ring[rows, NXY : NXY + 256]
        ring[rows, 256 + NXY :] = ring[rows, 256 : 256 + RING - 256 - NXY]

    close(ring0, 0, 24)
    b_all = -near_weight * 2.0 / half_range
    b_low = jnp.where(inside[0], b_all, 0.0)
    b_high = jnp.where(inside[2], b_all, 0.0)
    rings = (ring0, ring1)
    for order in range(4):
        a, b = 2 * order + 2, 22 - 2 * order
        now, other = (even, odd) if order % 2 == 0 else (odd, even)
        ring, following = rings[order % 2], rings[(order + 1) % 2]

        def block(n, _):
            window = ring[8 * a : 8 * b, pl.ds(pl.multiple_of(256 * n, 256), 768)]
            planar = jnp.dot(window, w_ref[lax.rem(n, 5)], preferred_element_type=F32)
            for l in range(2):
                cols = pl.ds(pl.multiple_of(256 * n + 128 * l, 128), 128)
                v = [now[8 * q : 8 * q + 8, cols] for q in range(a - 2, b + 2)]
                pending = None
                for q in range(a, b):
                    m = q - a + 2
                    near = v[m - 1] + v[m + 1]
                    far = v[m - 2] + v[m + 2]
                    t = planar[8 * (q - a) : 8 * (q - a) + 8, 128 * l : 128 * l + 128] + near - far * (1.0 / 16.0)
                    coef = b_low if q < 8 else (b_all if q < 16 else b_high)
                    new = scaled[8 * q : 8 * q + 8, cols] * v[m] + coef * t
                    if order == 0:
                        new = new * 0.5
                    else:
                        new = new - other[8 * q : 8 * q + 8, cols]
                    if order < 3:
                        other[8 * q : 8 * q + 8, cols] = new
                        if q % 2 == 0:
                            pending = new
                        else:
                            ring_cols = pl.ds(pl.multiple_of(256 * n + 128 * l + 256, 128), 128)
                            following[8 * q - 8 : 8 * q + 8, ring_cols] = jnp.concatenate(
                                [pending, new], axis=0).astype(BF16)
                    else:
                        rows = pl.ds(pl.multiple_of(64 * (2 * n + l) + 8 * (q - 8), 8), 8)
                        done[rows, :] = new
            return 0

        lax.fori_loop(0, 13, block, 0)
        if order < 3:
            close(following, a, b)
    def turn_out(t, _):
        cols = pl.ds(pl.multiple_of(128 * t, 128), 128)
        for o in range(8):
            out_ref[8 * o : 8 * o + 8, cols] = done[pl.ds(64 * t + o, 8, stride=8), :]
        return 0

    lax.fori_loop(0, 25, turn_out, 0)


def body(orbitals, rotation, potential, weights):
    vmem = pl.BlockSpec(memory_space=pltpu.VMEM)
    anyspace = pl.BlockSpec(memory_space=pl.ANY)
    packed = jax.ShapeDtypeStruct((16, 19, 16, LANES), BF16)
    plane = jax.ShapeDtypeStruct((8, NXY), F32)
    own, low, high, plow, phigh = pl.pallas_call(
        exchange_kernel,
        out_shape=[packed, packed, packed, plane, plane],
        in_specs=[vmem, vmem, anyspace],
        out_specs=[anyspace] * 5,
        scratch_shapes=[
            pltpu.VMEM((24 * 128, LANES), F32),
            pltpu.VMEM((24 * 128, LANES), F32),
            pltpu.VMEM((8, TILES + 1, 3, 16, LANES), BF16),
            pltpu.VMEM((8, TILES + 1, 3, 16, LANES), BF16),
            pltpu.VMEM((16, 19, 16, LANES), BF16),
            pltpu.VMEM((2, 192, 256), BF16),
            pltpu.SemaphoreType.DMA((8,)),
            pltpu.SemaphoreType.DMA((8,)),
            pltpu.SemaphoreType.DMA((16,)),
            pltpu.SemaphoreType.DMA((16,)),
            pltpu.SemaphoreType.DMA((2,)),
            pltpu.SemaphoreType.DMA((2,)),
            pltpu.SemaphoreType.DMA((2,)),
            pltpu.SemaphoreType.DMA((2,)),
            pltpu.SemaphoreType.DMA,
        ],
        compiler_params=pltpu.CompilerParams(
            collective_id=0, has_side_effects=True, vmem_limit_bytes=40 << 20),
        name="exchange",
    )(orbitals, rotation, potential)

    blocks = pl.BlockSpec((16, 6, 16, LANES), lambda g: (0, g, 0, 0))
    lasts = pl.BlockSpec((16, 1, 16, LANES), lambda g: (0, 18, 0, 0))
    whole = pl.BlockSpec((8, NXY), lambda g: (0, 0))
    out = pl.pallas_call(
        filter_kernel,
        grid=(3,),
        out_shape=jax.ShapeDtypeStruct((192, NXY), F32),
        in_specs=[blocks, lasts, blocks, lasts, blocks, lasts, whole, whole, whole,
                  pl.BlockSpec((5, 768, 256), lambda g: (0, 0, 0))],
        out_specs=pl.BlockSpec((64, NXY), lambda g: (g, 0)),
        scratch_shapes=[
            pltpu.VMEM((192, WIDE), F32),
            pltpu.VMEM((192, WIDE), F32),
            pltpu.VMEM((192, RING), BF16),
            pltpu.VMEM((192, RING), BF16),
            pltpu.VMEM((192, WIDE), F32),
            pltpu.VMEM((WIDE // LANES * 64, LANES), F32),
        ],
        compiler_params=pltpu.CompilerParams(vmem_limit_bytes=48 << 20),
        name="filter",
    )(own, own, low, low, high, high, potential, plow, phigh, weights)
    return out.reshape(24, 8, NXY)


def solution(mesh):
    in_specs = (P("band", None, "dom"), P("band", None), P("dom", None), P())
    out_specs = P("band", "dom", None)
    run = jax.shard_map(body, mesh=mesh, in_specs=in_specs, out_specs=out_specs, check_vma=False)

    def whole(orbitals, rotation, potential):
        return run(orbitals, rotation, potential, jnp.asarray(neighbour_weights(), BF16))

    return whole
```

time: 262 us -> 122 us (0.47)
  the two profiles are of different devices: /device:TPU:97 before, /device:TPU:54 now
where the time goes in v1:
time: 122 us
  Pallas kernels  119 us (98%)
  local copies, waits for them, and re-layouts  2.69 us (2%)
    pallas_call x1, Pallas kernels, body(): pl.pallas_call(exchange_kernel, out_shape=[packed, packed, packed, plane,...  74.9 us
    pallas_call x1, Pallas kernels, body(): pl.pallas_call(filter_kernel, grid=(3,), out_shape=jax.ShapeDtypeStruct((...  43.8 us
    unnamed x9, local copies, waits for them, and re-layouts  2.69 us

profile of v1, /device:TPU:54, one launch (start us, length us, event | category | flops | bytes accessed | tf_op | source)
XLA Modules:
  0.0 121.5 jit_solution(445684581134672891)
XLA Ops:
  0.0 0.0 copy-start.3
  0.0 0.0 copy-start
  0.0 1.8 %copy.5.orb_ref = bf16[24,128,200]{2,1,0:T(8,128)(2,1)S(1)} copy(bf16[24,128,200]{1,2,0:T(8,128)(2,1)} %param.4) | data formatting | bytes 2457600 | tf_op args[0]
  1.8 0.0 copy-done.3
  1.8 0.0 copy-start.1
  1.8 0.9 copy-done.1
  2.7 0.0 copy-start.2
  2.7 74.9 %exchange.1 = (bf16[16,19,16,128]{3,2,1,0:T(8,128)(2,1)S(1)}, bf16[16,19,16,128]{3,2,1,0:T(8,128)(2,1)S(1)}, bf16[16,19,16,128]{3,2,1,0:T(8,128)(2,1)S(1)}, f32[8,3200]{1,0:T(8,128)S(1)}, f32[8,3200]{1,0:T(8,128)S(1)}) custom-call(bf16[24,128,200]{2,1,0:T(8,128)(2,1)S(1)} %copy.5.orb_ref, bf16[24,192]{1,0:T(8,128)(2,1)S(1)} %copy-done.3, f32[8,3200]{1,0:T(8,128)S(1)} %copy-done.1), custom_call_target="tpu_custom_call" | custom-call | tf_op jit(solution)/shard_map/exchange/pallas_call | solution.py:376
  77.6 0.0 copy-done
  77.7 0.0 copy-done.2
  77.7 43.8 %filter.1 = f32[192,3200]{1,0:T(8,128)} custom-call(bf16[16,19,16,128]{3,2,1,0:T(8,128)(2,1)S(1)} %get-tuple-element.10.own_ref.own_x, bf16[16,19,16,128]{3,2,1,0:T(8,128)(2,1)S(1)} %get-tuple-element.10.own_ref.own_x, bf16[16,19,16,128]{3,2,1,0:T(8,128)(2,1)S(1)} %get-tuple-element.11.low_ref.low_x, ...), custom_call_target="tpu_custom_call" | custom-call | tf_op jit(solution)/shard_map/filter/pallas_call | solution.py:406
Async XLA Ops:
  0.0 1.8 %copy-start.3 = (bf16[24,192]{1,0:T(8,128)(2,1)S(1)}, bf16[24,192]{1,0:T(8,128)(2,1)}, u32[]{:S(2)}) copy-start(bf16[24,192]{1,0:T(8,128)(2,1)} %rot_ref.1) | copy-start | bytes 27652
  0.0 77.6 %copy-start = (bf16[5,768,256]{2,1,0:T(8,128)(2,1)S(1)}, bf16[5,768,256]{2,1,0:T(8,128)(2,1)}, u32[]{:S(2)}) copy-start(bf16[5,768,256]{2,1,0:T(8,128)(2,1)} %constant.2.clone.w_ref) | copy-start | bytes 5898244
  1.8 0.9 copy-start.1
  2.7 74.9 %copy-start.2 = (f32[8,3200]{1,0:T(8,128)S(1)}, f32[8,3200]{1,0:T(8,128)}, u32[]{:S(2)}) copy-start(f32[8,3200]{1,0:T(8,128)} %pot_ref.3) | copy-start | bytes 307204

commit v2 on v1

--- a/solution.py
+++ b/solution.py
@@ -121,10 +121,20 @@
             send1[k, t, 0] = a[:16].astype(BF16)
             send1[k, t, 1] = b[:16].astype(BF16)
             send1[k, t, 2] = jnp.concatenate([a[16:], b[16:]], axis=0).astype(BF16)
-        copy1(k, band, hh * 4 + yy).start()
         return 0
 
     lax.fori_loop(0, 8, pack, 0)
+
+    def post1(i, _):
+        k = lax.rem(i, 8)
+        part = pl.ds(2 * (i // 8), 2)
+        hh, yy = partner(k)
+        pltpu.make_async_remote_copy(
+            src_ref=send1.at[k, part], dst_ref=recv1.at[band, part], send_sem=s1.at[k], recv_sem=r1.at[band],
+            device_id={"band": hh * 4 + yy, "dom": mirror}, device_id_type=MESH).start()
+        return 0
+
+    lax.fori_loop(0, 56, post1, 0)
     for k in range(8):
         copy1(k, k, band).wait_recv()
 
@@ -325,9 +335,15 @@
         now, other = (even, odd) if order % 2 == 0 else (odd, even)
         ring, following = rings[order % 2], rings[(order + 1) % 2]
 
-        def block(n, _):
-            window = ring[8 * a : 8 * b, pl.ds(pl.multiple_of(256 * n, 256), 768)]
-            planar = jnp.dot(window, w_ref[lax.rem(n, 5)], preferred_element_type=F32)
+        def sweep(w, _, count):
+            windows = [
+                ring[8 * a : 8 * b, pl.ds(pl.multiple_of(256 * w + 1280 * i, 256), 768)] for i in range(count)]
+            planar = jnp.dot(jnp.concatenate(windows, axis=0), w_ref[w], preferred_element_type=F32)
+            for i in range(count):
+                block(w + 5 * i, planar[8 * (b - a) * i : 8 * (b - a) * (i + 1)])
+            return 0
+
+        def block(n, planar):
             for l in range(2):
                 cols = pl.ds(pl.multiple_of(256 * n + 128 * l, 128), 128)
                 v = [now[8 * q : 8 * q + 8, cols] for q in range(a - 2, b + 2)]
@@ -354,9 +370,9 @@
                     else:
                         rows = pl.ds(pl.multiple_of(64 * (2 * n + l) + 8 * (q - 8), 8), 8)
                         done[rows, :] = new
-            return 0
-
-        lax.fori_loop(0, 13, block, 0)
+
+        lax.fori_loop(0, 3, functools.partial(sweep, count=3), 0)
+        lax.fori_loop(3, 5, functools.partial(sweep, count=2), 0)
         if order < 3:
             close(following, a, b)
     def turn_out(t, _):

time: 122 us -> 93.9 us (0.77)
  the two profiles are of different devices: /device:TPU:54 before, /device:TPU:97 now
where the time goes in v2:
time: 93.9 us; the launch traced here: 92.2 us
  Pallas kernels  89.4 us (95%)
  local copies, waits for them, and re-layouts  2.69 us (3%)
    pallas_call x1, Pallas kernels, body(): pl.pallas_call(exchange_kernel, out_shape=[packed, packed, packed, plane,...  64 us
    pallas_call x1, Pallas kernels, body(): pl.pallas_call(filter_kernel, grid=(3,), out_shape=jax.ShapeDtypeStruct((...  25.5 us
    unnamed x9, local copies, waits for them, and re-layouts  2.69 us

profile of v2, /device:TPU:97, one launch (start us, length us, event | category | flops | bytes accessed | tf_op | source)
XLA Modules:
  0.0 92.2 jit_solution(10942796251372671194)
XLA Ops:
  0.0 0.0 copy-start.3
  0.0 0.0 copy-start
  0.0 1.8 %copy.5.orb_ref = bf16[24,128,200]{2,1,0:T(8,128)(2,1)S(1)} copy(bf16[24,128,200]{1,2,0:T(8,128)(2,1)} %param.4) | data formatting | bytes 2457600 | tf_op args[0]
  1.8 0.0 copy-done.3
  1.8 0.0 copy-start.1
  1.8 0.9 copy-done.1
  2.7 0.0 copy-start.2
  2.7 64.0 %exchange.1 = (bf16[16,19,16,128]{3,2,1,0:T(8,128)(2,1)S(1)}, bf16[16,19,16,128]{3,2,1,0:T(8,128)(2,1)S(1)}, bf16[16,19,16,128]{3,2,1,0:T(8,128)(2,1)S(1)}, f32[8,3200]{1,0:T(8,128)S(1)}, f32[8,3200]{1,0:T(8,128)S(1)}) custom-call(bf16[24,128,200]{2,1,0:T(8,128)(2,1)S(1)} %copy.5.orb_ref, bf16[24,192]{1,0:T(8,128)(2,1)S(1)} %copy-done.3, f32[8,3200]{1,0:T(8,128)S(1)} %copy-done.1), custom_call_target="tpu_custom_call" | custom-call | tf_op jit(solution)/shard_map/exchange/pallas_call | solution.py:392
  66.7 0.0 copy-done
  66.7 0.0 copy-done.2
  66.7 25.5 %filter.1 = f32[192,3200]{1,0:T(8,128)} custom-call(bf16[16,19,16,128]{3,2,1,0:T(8,128)(2,1)S(1)} %get-tuple-element.10.own_ref.own_x, bf16[16,19,16,128]{3,2,1,0:T(8,128)(2,1)S(1)} %get-tuple-element.10.own_ref.own_x, bf16[16,19,16,128]{3,2,1,0:T(8,128)(2,1)S(1)} %get-tuple-element.11.low_ref.low_x, ...), custom_call_target="tpu_custom_call" | custom-call | tf_op jit(solution)/shard_map/filter/pallas_call | solution.py:422
Async XLA Ops:
  0.0 1.8 %copy-start.3 = (bf16[24,192]{1,0:T(8,128)(2,1)S(1)}, bf16[24,192]{1,0:T(8,128)(2,1)}, u32[]{:S(2)}) copy-start(bf16[24,192]{1,0:T(8,128)(2,1)} %rot_ref.1) | copy-start | bytes 27652
  0.0 66.7 %copy-start = (bf16[5,768,256]{2,1,0:T(8,128)(2,1)S(1)}, bf16[5,768,256]{2,1,0:T(8,128)(2,1)}, u32[]{:S(2)}) copy-start(bf16[5,768,256]{2,1,0:T(8,128)(2,1)} %constant.2.clone.w_ref) | copy-start | bytes 5898244
  1.8 0.9 copy-start.1
  2.7 64.0 %copy-start.2 = (f32[8,3200]{1,0:T(8,128)S(1)}, f32[8,3200]{1,0:T(8,128)}, u32[]{:S(2)}) copy-start(f32[8,3200]{1,0:T(8,128)} %pot_ref.3) | copy-start | bytes 307204

commit v3 on v0

v3 whole, which is shorter than its diff:
```python
import jax
import jax.numpy as jnp
import numpy as np
from jax import lax
from jax.experimental import pallas as pl
from jax.experimental.pallas import tpu as pltpu
from jax.sharding import PartitionSpec as P

NXY = 3200
MESH = pl.DeviceIdType.MESH
F32 = jnp.float32
BF16 = jnp.bfloat16
LANES = 128

potential_offset = 0.5
near_weight = 2.0 / 3.0
half_range = 4.25


def target_domain(h, y, z, c, half):
    return lax.rem(h + half, 2) * 8 + lax.rem(z + y + c + 2 * half, 4) * 2 + half


def kernel(
    orb_hbm, rot_hbm, pot_hbm, wy_ref,
    out_hbm,
    orb, rot, pot, wide, send1, recv1, send2, weights,
    own, low, high, pown, plow, phigh,
    even, odd, ring0, ring1, scaled, done, result,
    s1, r1, s2, r2, sh, rh, sp, rp, ls, li, lo,
):
    band, dom = lax.axis_index("band"), lax.axis_index("dom")
    h, y = band // 4, lax.rem(band, 4)
    x, z, c = dom // 8, lax.rem(dom // 2, 4), lax.rem(dom, 2)
    mirror = (1 - x) * 8 + z * 2 + c
    has_low, has_high = dom > 0, dom < 15
    up, down = lax.rem(dom + 1, 16), lax.rem(dom + 15, 16)

    def partner(k):
        return lax.rem(h + k // 4, 2) * 4 + lax.rem(y + lax.rem(k, 4), 4)

    def load(i):
        return pltpu.make_async_copy(orb_hbm.at[pl.ds(4 * i, 4)], orb.at[pl.ds(4 * i, 4)], li.at[i])

    load_rot = pltpu.make_async_copy(rot_hbm, rot, li.at[6])
    load_pot = pltpu.make_async_copy(pot_hbm, pot, li.at[7])
    for i in range(6):
        load(i).start()
    load_rot.start()
    load_pot.start()

    barrier = pltpu.get_barrier_semaphore()

    def greet(b, d):
        pl.semaphore_signal(barrier, inc=1, device_id={"band": b, "dom": d}, device_id_type=MESH)

    greet(band, up)
    greet(band, down)
    lane = lax.broadcasted_iota(jnp.int32, (8, LANES), 1)
    block = lane // 16
    lane24 = lax.broadcasted_iota(jnp.int32, (24, LANES), 1)
    block24 = lane24 // 16

    for i in range(6):
        load(i).wait()

        def widen(o, _):
            k = lax.rem(o, 8)
            half = jnp.where(o < 16, 0, 1)
            greet(partner(k), jnp.where(o < 8, mirror, target_domain(h, y, z, c, half)))

            @pl.when(o < 16)
            def _():
                qz, qc = lax.rem(o // 2, 4), lax.rem(o, 2)
                greet(lax.rem(x + c, 2) * 4 + lax.rem(z - qz - qc - 2 * c + 16, 4), o)

            rows = pl.ds(pl.multiple_of(o * 128, 128), 128)
            v = orb[o].astype(F32)
            a, b = v[:, :LANES], jnp.concatenate([v[:, LANES:], v[:, : 256 - 200]], axis=1)
            wide[0, rows, :] = jnp.where(c == 0, a, jnp.concatenate([v[:, 8:128], v[:, 128:136]], axis=1))
            wide[1, rows, :] = jnp.where(
                c == 0, b, jnp.concatenate([v[:, 136:200], v[:, : 128 - 64]], axis=1))
            return 0

        lax.fori_loop(4 * i, 4 * i + 4, widen, 0)

    load_rot.wait()
    r = rot[...].astype(F32)
    r_left = r[:, :LANES]
    r_right = jnp.concatenate([r[:, LANES:], r[:, : 256 - 192]], axis=1)

    def pack(t, u, half, k, own_turn):
        to = partner(k)
        first = target_domain(to // 4, lax.rem(to, 4), z, c, half) * 8
        v = None
        for zz in range(8):
            s = pltpu.roll(wide[u // 8, pl.ds(first + zz, 24, stride=128), :], 16 * zz, 1)
            v = s if v is None else jnp.where(block24 == lax.rem(u + zz, 8), s, v)
        return pltpu.roll(v, own_turn, 1)

    def put(k, t, a, b):
        send1[k, t, 0] = a[:16].astype(BF16)
        send1[k, t, 1] = b[:16].astype(BF16)
        send1[k, t, 2] = jnp.concatenate([a[16:], b[16:]], axis=0).astype(BF16)

    def copy1(slot, source, part, to):
        rows = pl.ds(2 * part, 2)
        return pltpu.make_async_remote_copy(
            src_ref=send1.at[slot, rows], dst_ref=recv1.at[source, rows],
            send_sem=s1.at[part, slot], recv_sem=r1.at[part, source],
            device_id={"band": to, "dom": mirror}, device_id_type=MESH)

    turn = (dom // 2) * 16
    pl.semaphore_wait(barrier, 42)

    def ends(k, _):
        put(k, 0, *[pack(0, 12, half, k, turn + 8 * c) for half in range(2)])
        put(k, 1, r_left, r_right)
        copy1(k, band, 0, partner(k)).start()
        return 0

    lax.fori_loop(0, 8, ends, 0)

    def units(i, _):
        part, k = i // 8 + 1, lax.rem(i, 8)
        for j in range(2):
            u = 2 * part - 2 + j
            put(k, u + 2, *[pack(u + 2, u, half, k, turn) for half in range(2)])
        copy1(k, band, part, partner(k)).start()
        return 0

    lax.fori_loop(0, 48, units, 0)

    load_pot.wait()
    for t in range(25):
        v = None
        for p in range(8):
            tile = (25 * p + t) // 8
            s = pot[:, 128 * tile : 128 * tile + 128]
            v = s if v is None else jnp.where(block == (p + t) % 8, s, v)
        if t % 8:
            v = pltpu.roll(v, 128 - 16 * (t % 8), 1)
        pown[t] = (v - potential_offset) * (2.0 / half_range)

    pot_copies = []
    for i, (dst, to, ok) in enumerate(((plow, up, has_high), (phigh, down, has_low))):
        cp = pltpu.make_async_remote_copy(
            src_ref=pown, dst_ref=dst, send_sem=sp.at[i], recv_sem=rp.at[i],
            device_id={"band": band, "dom": to}, device_id_type=MESH)
        pot_copies.append(cp)
        pl.when(ok)(cp.start)

    for k in range(8):
        copy1(k, k, 0, band).wait_recv()
    zero = jnp.zeros((8, 2 * LANES), F32)
    first_rows = jnp.concatenate([
        recv1[:, 1, 0].astype(F32).reshape(128, LANES),
        recv1[:, 1, 1].astype(F32).reshape(128, LANES)], axis=1)
    for half in range(2):
        rows = [first_rows]
        for k in range(8):
            m = recv1[k, 1, 2].astype(F32)
            m = jnp.concatenate([m[:8], m[8:]], axis=1)
            rows += [m, zero] if half == 0 else [zero, m]
        weights[half] = jnp.transpose(jnp.concatenate(rows, axis=0))[:192].astype(BF16)

    def rhs(t, half):
        return jnp.concatenate(
            [recv1[:, t, half].reshape(128, LANES), recv1[:, t, 2].reshape(128, LANES)], axis=0)

    is_odd_half = lax.rem(lane // 8, 2)
    for half in range(2):
        out = jnp.dot(weights[half], rhs(0, half), preferred_element_type=F32)
        for b in range(8):
            v = out[24 * b : 24 * b + 24]
            first = jnp.where(is_odd_half == c, v[:8], pltpu.roll(v[16:], jnp.where(c == 0, 8, 120), 1))
            send2[half * 8 + b, 0, 6] = jnp.concatenate([first, v[8:16]], axis=0).astype(BF16)

    def rotate(part, _):
        for k in range(8):
            copy1(k, k, part, band).wait_recv()
        for half in range(2):
            both = jnp.concatenate([rhs(2 * part, half), rhs(2 * part + 1, half)], axis=1)
            out = jnp.dot(weights[half], both, preferred_element_type=F32)
            for b in range(8):
                for g in range(3):
                    v = out[24 * b + 8 * g : 24 * b + 8 * g + 8]
                    v = jnp.concatenate([v[:, :LANES], v[:, LANES:]], axis=0)
                    send2[half * 8 + b, g, part - 1] = v.astype(BF16)
        return 0

    lax.fori_loop(1, 7, rotate, 0)

    def tiles(g):
        return pl.ds(0, 7 if g == 0 else 6)

    def copy2(slot, source, g, b, d):
        return pltpu.make_async_remote_copy(
            src_ref=send2.at[slot, g, tiles(g)], dst_ref=own.at[g, source, tiles(g)],
            send_sem=s2.at[g, slot], recv_sem=r2.at[g, source],
            device_id={"band": b, "dom": d}, device_id_type=MESH)

    def keep(slot, source, g):
        return pltpu.make_async_copy(send2.at[slot, g, tiles(g)], own.at[g, source, tiles(g)], ls.at[g])

    def is_self(half):
        return target_domain(h, y, z, c, half) == dom

    for g in range(3):
        def post(i, _):
            half, k = i // 8, lax.rem(i, 8)
            to, to_dom = partner(k), target_domain(h, y, z, c, half)
            here = jnp.logical_and(to_dom == dom, k == 0)

            @pl.when(jnp.logical_not(here))
            def _():
                copy2(half * 8 + to, mirror, g, to, to_dom).start()

            @pl.when(here)
            def _():
                keep(half * 8 + to, mirror, g).start()

            return 0

        lax.fori_loop(0, 16, post, 0)

    self_sent = jnp.logical_or(is_self(0), is_self(1))

    def halo(i, g):
        dst, to = ((low, up), (high, down))[i]
        return pltpu.make_async_remote_copy(
            src_ref=own.at[g, :, tiles(g)], dst_ref=dst.at[g, :, tiles(g)], send_sem=sh.at[i, g], recv_sem=rh.at[i, g],
            device_id={"band": band, "dom": to}, device_id_type=MESH)

    def arrive(g):
        def one(q, _):
            here = jnp.logical_and(self_sent, mirror == q)

            @pl.when(jnp.logical_not(here))
            def _():
                copy2(q, q, g, band, dom).wait_recv()

            @pl.when(here)
            def _():
                keep(0, q, g).wait()

            return 0

        lax.fori_loop(0, 16, one, 0)
        pl.when(has_high)(halo(0, g).start)
        pl.when(has_low)(halo(1, g).start)

    inside = (has_low, None, has_high)
    for i, ok_send, ok_recv in ((0, has_high, has_low), (1, has_low, has_high)):
        pl.when(ok_recv)(pot_copies[i].wait_recv)

    for region, ref in enumerate((plow, pown, phigh)):
        def spread(t, _):
            v = ref[t]
            if inside[region] is not None:
                v = jnp.where(inside[region], v, 0.0)
            for zz in range(8):
                rows = slice(64 * region + 8 * zz, 64 * region + 8 * zz + 8)
                scaled[t, rows, :] = jnp.broadcast_to(v[zz : zz + 1], (8, LANES))
            return 0

        lax.fori_loop(0, 25, spread, 0)

    b_all = -near_weight * 2.0 / half_range
    b_low = jnp.where(has_low, b_all, 0.0)
    b_high = jnp.where(has_high, b_all, 0.0)
    rings = (ring0, ring1)

    def to_ring(ring, t, rows, v):
        xl, yh = t // 5, t % 5
        for pos in {0: (1, 6), 1: (2, 7), 4: (5, 0)}.get(yh, (yh + 1,)):
            ring[xl, rows, 128 * pos : 128 * pos + 128] = v

    def unpack(region, ref, g):
        def finish(t, zz, pair):
            if inside[region] is not None:
                pair = [jnp.where(inside[region], v, 0.0) for v in pair]
            v = jnp.concatenate(pair, axis=0)
            rows = slice(64 * region + 8 * zz, 64 * region + 8 * zz + 16)
            even[t, rows, :] = v
            to_ring(ring0, t, rows, v.astype(BF16))

        for e in range(2):
            for i in range(6):
                src = [ref[g, 2 * p + e, i].astype(F32) for p in range(8)]
                for j in range(2):
                    u = 2 * i + j
                    for zz in range(0, 8, 2):
                        pair = []
                        for s in (u + zz, u + zz + 1):
                            v = src[0][8 * j : 8 * j + 8]
                            for p in range(1, 8):
                                v = jnp.where(block == (s + p) % 8, src[p][8 * j : 8 * j + 8], v)
                            pair.append(pltpu.roll(v, 128 - 16 * (s % 8), 1) if s % 8 else v)
                        finish(13 * e + u, zz, pair)
        src = []
        for d in range(16):
            v = ref[0, d, 6].astype(F32)
            v = jnp.where(g == 1, v[8:], v[:8])
            src.append(jnp.where(g == 2, pltpu.roll(v, 8 if d % 2 else 120, 1), v))
        for zz in range(0, 8, 2):
            pair = []
            for s in (12 + zz, 13 + zz):
                v = src[0]
                for d in range(1, 16):
                    v = jnp.where(lane // 8 == 2 * ((s + d // 2) % 8) + d % 2, src[d], v)
                pair.append(pltpu.roll(v, 128 - 16 * (s % 8), 1) if s % 8 else v)
            finish(12, zz, pair)

    def step(order):
        a, b = 2 * order + 2, 22 - 2 * order
        now, other = (even, odd) if order % 2 == 0 else (odd, even)
        ring, following = rings[order % 2], rings[(order + 1) % 2]
        count = 8 * (b - a)
        for n in range(3):
            window = jnp.concatenate(
                [ring[xl, 8 * a : 8 * b, 256 * n : 256 * n + 512] for xl in range(5)], axis=0)
            width = 256 if n < 2 else 128
            planar = jnp.dot(window, wy_ref[:, :width], preferred_element_type=F32)
            for l in range(width // 128):
                yh = 2 * n + l
                v = {q: [now[5 * xl + yh, 8 * q : 8 * q + 8, :] for xl in range(5)] for q in range(a - 2, b + 2)}
                pending = None
                for q in range(a, b):
                    m = v[q]
                    before = [pltpu.roll(m[3], 16, 1), pltpu.roll(m[4], 16, 1)]
                    after = [pltpu.roll(m[0], 112, 1), pltpu.roll(m[1], 112, 1)]
                    line = before + m + after
                    coef = b_low if q < 8 else (b_all if q < 16 else b_high)
                    news = []
                    for xl in range(5):
                        t = 5 * xl + yh
                        near = (line[xl + 1] + line[xl + 3]) + (v[q - 1][xl] + v[q + 1][xl])
                        far = (line[xl] + line[xl + 4]) + (v[q - 2][xl] + v[q + 2][xl])
                        rows = slice(8 * q, 8 * q + 8)
                        first = count * xl + 8 * (q - a)
                        total = planar[first : first + 8, 128 * l : 128 * l + 128] + near - far * (1.0 / 16.0)
                        new = scaled[t, rows, :] * m[xl] + coef * total
                        if order == 0:
                            new = new * 0.5
                        else:
                            new = new - other[t, rows, :]
                        if order < 3:
                            other[t, rows, :] = new
                        else:
                            done[64 * t + 8 * (q - 8) : 64 * t + 8 * (q - 8) + 8, :] = new
                        news.append(new)
                    if order < 3:
                        if q % 2:
                            for xl in range(5):
                                to_ring(following, 5 * xl + yh, slice(8 * q - 8, 8 * q + 8),
                                        jnp.concatenate([pending[xl], news[xl]], axis=0).astype(BF16))
                        pending = news

    def write(g):
        return pltpu.make_async_copy(result.at[g], out_hbm.at[pl.ds(pl.multiple_of(64 * g, 64), 64)], lo.at[g])

    arrive(0)

    def group(g, _):
        for nxt in (1, 2):
            @pl.when(g == nxt - 1)
            def _():
                arrive(nxt)

        for now in range(3):
            @pl.when(g == now)
            def _():
                pl.when(has_low)(halo(0, now).wait_recv)
                pl.when(has_high)(halo(1, now).wait_recv)

        for region, ref in enumerate((low, own, high)):
            unpack(region, ref, g)
        for order in range(4):
            step(order)

        def turn_out(o, _):
            v = []
            for t in range(25):
                s = done[pl.ds(64 * t + o, 8, stride=8), :]
                v.append(pltpu.roll(s, 16 * (t % 8), 1) if t % 8 else s)
            rows = pl.ds(pl.multiple_of(8 * o, 8), 8)
            for tau in range(25):
                s = v[8 * tau % 25]
                for beta in range(1, 8):
                    s = jnp.where(block == beta, v[(8 * tau + beta) % 25], s)
                result[g, rows, 128 * tau : 128 * tau + 128] = s
            return 0

        lax.fori_loop(0, 8, turn_out, 0)
        write(g).start()
        return 0

    lax.fori_loop(0, 3, group, 0)

    def drain1(i, _):
        copy1(lax.rem(i, 8), 0, i // 8, band).wait_send()
        return 0

    lax.fori_loop(0, 56, drain1, 0)
    for g in range(3):
        def drain2(slot, _):
            here = jnp.logical_and(target_domain(h, y, z, c, slot // 8) == dom, lax.rem(slot, 8) == band)

            @pl.when(jnp.logical_not(here))
            def _():
                copy2(slot, 0, g, band, dom).wait_send()

            return 0

        lax.fori_loop(0, 16, drain2, 0)
        pl.when(has_high)(halo(0, g).wait_send)
        pl.when(has_low)(halo(1, g).wait_send)
    pl.when(has_high)(pot_copies[0].wait_send)
    pl.when(has_low)(pot_copies[1].wait_send)
    for g in range(3):
        write(g).wait()


def y_weights():
    out = np.zeros((512, 256), np.float32)
    for col in range(256):
        j, p, yl = col // 128, col % 128 // 16, col % 16
        for step, value in ((1, 1.0), (2, -1.0 / 16.0)):
            for sign in (-1, 1):
                at = yl + sign * step
                out[128 * (1 + j + at // 16) + 16 * p + at % 16, col] += value
    return out


def body(orbitals, rotation, potential, weights):
    anyspace = pl.BlockSpec(memory_space=pl.ANY)
    dma = pltpu.SemaphoreType.DMA
    group = pltpu.VMEM((3, 16, 7, 16, LANES), BF16)
    plane = pltpu.VMEM((25, 8, LANES), F32)
    field = pltpu.VMEM((25, 192, LANES), F32)
    ring = pltpu.VMEM((5, 192, 1024), BF16)
    parts = pltpu.VMEM((8, 14, 3, 16, LANES), BF16)
    out = pl.pallas_call(
        kernel,
        out_shape=jax.ShapeDtypeStruct((192, NXY), F32),
        in_specs=[anyspace, anyspace, anyspace, pl.BlockSpec(memory_space=pltpu.VMEM)],
        out_specs=anyspace,
        scratch_shapes=[
            pltpu.VMEM((24, 128, 200), BF16),
            pltpu.VMEM((24, 192), BF16),
            pltpu.VMEM((8, NXY), F32),
            pltpu.VMEM((2, 24 * 128, LANES), F32),
            parts, parts,
            pltpu.VMEM((16, 3, 7, 16, LANES), BF16),
            pltpu.VMEM((2, 192, 256), BF16),
            group, group, group,
            plane, plane, plane,
            field, field, ring, ring, field,
            pltpu.VMEM((25 * 64, LANES), F32),
            pltpu.VMEM((3, 64, NXY), F32),
            dma((7, 8)), dma((7, 8)), dma((3, 16)), dma((3, 16)),
            dma((2, 3)), dma((2, 3)), dma((2,)), dma((2,)), dma((3,)), dma((8,)), dma((3,)),
        ],
        compiler_params=pltpu.CompilerParams(
            collective_id=0, has_side_effects=True, vmem_limit_bytes=56 << 20),
        name="rotate_and_filter",
    )(orbitals, rotation, potential, weights)
    return out.reshape(24, 8, NXY)


def solution(mesh):
    in_specs = (P("band", None, "dom"), P("band", None), P("dom", None), P())
    out_specs = P("band", "dom", None)
    run = jax.shard_map(body, mesh=mesh, in_specs=in_specs, out_specs=out_specs, check_vma=False)

    def whole(orbitals, rotation, potential):
        return run(orbitals, rotation, potential, jnp.asarray(y_weights(), BF16))

    return whole
```

time: 262 us -> 86.6 us (0.33); the launches traced: 257 us -> 85.1 us
  Pallas kernels: 0 us -> 79.3 us
  blocking collectives: 59.9 us -> 0 us
  waiting for transfers between devices: 56.3 us -> 0 us
  local copies, waits for them, and re-layouts: 61.7 us -> 5.8 us
  starting transfers between devices: 39.1 us -> 0 us
  other arithmetic: 38.1 us -> 0 us
    pallas_call x0 -> x1, Pallas kernels: none -> 79.3 us  [body(): pl.pallas_call(kernel, out_shape=jax.ShapeDtypeStruct((192, NXY), F32), i...]
    all_gather x1 -> x0, blocking collectives: 42.8 us -> none  [body(): full_matrix = lax.all_gather(rotation, 'band', axis=0, tiled=True)]
    slice x52 -> x0, local copies, waits for them, and re-layouts: 40.8 us -> none  [the longest x16 11 us: shift_columns(): jnp.roll(values, offset, -1)]
    ppermute x8 -> x0, waiting for transfers between devices: 34.4 us -> none  [the longest x4 29 us: extended_2(): lax.ppermute(head, axis, [((i + 1) % count, i) for i in range(ends)])]
    sub x3 -> x0, other arithmetic: 27.6 us -> none  [body(): following = 2.0 / half_range * operated - previous]
    all_to_all x2 -> x0, waiting for transfers between devices: 21.9 us -> none  [the longest x1 21.9 us: body(): lax.all_to_all(lax.all_to_all(rotated, 'band', split_axis=0, concat_axis=...]
    all_to_all x2 -> x0, starting transfers between devices: 20.9 us -> none  [the longest x1 14.3 us: body(): lax.all_to_all(lax.all_to_all(rotated, 'band', split_axis=0, concat_axis=...]
    ppermute x8 -> x0, starting transfers between devices: 18.2 us -> none  [the longest x4 10.3 us: extended_2(): lax.ppermute(head, axis, [((i + 1) % count, i) for i in range(ends)])]
  transfers between devices with their start and end apart: 10 -> 0, of which waited for: 8 -> 0; matrix products, arithmetic and copies ran while one was open for 4% -> 0% of each run, Pallas kernels for 0% -> 0%
where the time goes in v3:
time: 86.6 us; the launch traced here: 85.1 us
  Pallas kernels  79.3 us (92%)
  local copies, waits for them, and re-layouts  5.8 us (7%)
    pallas_call x1, Pallas kernels, body(): pl.pallas_call(kernel, out_shape=jax.ShapeDtypeStruct((192, NXY), F32), i...  79.3 us
    unnamed x2, local copies, waits for them, and re-layouts  5.8 us

profile of v3, /device:TPU:97, one launch (start us, length us, event | category | flops | bytes accessed | tf_op | source)
XLA Modules:
  0.0 85.1 jit_solution(7693773978450713523)
XLA Ops:
  0.0 2.5 %copy.5.orb_hbm = bf16[24,128,200]{2,1,0:T(8,128)(2,1)} copy(bf16[24,128,200]{1,2,0:T(8,128)(2,1)} %param.4) | data formatting | bytes 2457600 | tf_op args[0]
  2.5 79.3 %rotate_and_filter.1 = f32[192,3200]{1,0:T(8,128)} custom-call(bf16[24,128,200]{2,1,0:T(8,128)(2,1)} %copy.5.orb_hbm, bf16[24,192]{1,0:T(8,128)(2,1)} %rot_hbm.1, f32[8,3200]{1,0:T(8,128)} %pot_hbm.1, bf16[512,256]{1,0:T(8,128)(2,1)} %constant.2.clone.wy_ref), custom_call_target="tpu_custom_call" | custom-call | tf_op jit(solution)/shard_map/rotate_and_filter/pallas_call | solution.py:444
  81.8 3.3 %copy.7 = f32[24,8,3200]{2,1,0:T(8,128)} copy(f32[24,8,3200]{2,1,0:T(8,128)} %bitcast.1) | data formatting | bytes 4915200

commit v4 on v3

--- a/solution.py
+++ b/solution.py
@@ -24,9 +24,9 @@
 def kernel(
     orb_hbm, rot_hbm, pot_hbm, wy_ref,
     out_hbm,
-    orb, rot, pot, wide, send1, recv1, send2, weights,
+    orb, rot, pot, wide, planes, send1, recv1, send2, weights,
     own, low, high, pown, plow, phigh,
-    even, odd, ring0, ring1, scaled, done, result,
+    even, odd, ring0, ring1, scaled, done,
     s1, r1, s2, r2, sh, rh, sp, rp, ls, li, lo,
 ):
     band, dom = lax.axis_index("band"), lax.axis_index("dom")
@@ -56,6 +56,12 @@
 
     greet(band, up)
     greet(band, down)
+    for k in range(8):
+        greet(partner(k), mirror)
+    for q in range(16):
+        qz, qc = (q // 2) % 4, q % 2
+        greet(lax.rem(x + c, 2) * 4 + lax.rem(z - qz - qc - 2 * c + 16, 4), q)
+    turn = (dom // 2) * 16
     lane = lax.broadcasted_iota(jnp.int32, (8, LANES), 1)
     block = lane // 16
     lane24 = lax.broadcasted_iota(jnp.int32, (24, LANES), 1)
@@ -65,38 +71,37 @@
         load(i).wait()
 
         def widen(o, _):
-            k = lax.rem(o, 8)
-            half = jnp.where(o < 16, 0, 1)
-            greet(partner(k), jnp.where(o < 8, mirror, target_domain(h, y, z, c, half)))
-
-            @pl.when(o < 16)
-            def _():
-                qz, qc = lax.rem(o // 2, 4), lax.rem(o, 2)
-                greet(lax.rem(x + c, 2) * 4 + lax.rem(z - qz - qc - 2 * c + 16, 4), o)
-
             rows = pl.ds(pl.multiple_of(o * 128, 128), 128)
             v = orb[o].astype(F32)
-            a, b = v[:, :LANES], jnp.concatenate([v[:, LANES:], v[:, : 256 - 200]], axis=1)
-            wide[0, rows, :] = jnp.where(c == 0, a, jnp.concatenate([v[:, 8:128], v[:, 128:136]], axis=1))
-            wide[1, rows, :] = jnp.where(
-                c == 0, b, jnp.concatenate([v[:, 136:200], v[:, : 128 - 64]], axis=1))
+            v = jnp.where(c == 0, v, jnp.concatenate([v[8:], v[:8]], axis=0))
+            for j, w in enumerate((v[:LANES], jnp.concatenate([v[LANES:], v[: 256 - 200]], axis=0))):
+                wide[j, rows, :] = jnp.transpose(w)
             return 0
 
         lax.fori_loop(4 * i, 4 * i + 4, widen, 0)
 
+    def by_plane(d, _):
+        for zz in range(8):
+            first = pl.multiple_of(192 * d + 24 * zz, 8)
+            for j in range(2):
+                v = wide[j, pl.ds(8 * d + zz, 24, stride=128), :]
+                planes[j, pl.ds(first, 24), :] = pltpu.roll(v, lax.rem(turn + 16 * zz, 128), 1)
+        return 0
+
+    lax.fori_loop(0, 16, by_plane, 0)
     load_rot.wait()
     r = rot[...].astype(F32)
     r_left = r[:, :LANES]
     r_right = jnp.concatenate([r[:, LANES:], r[:, : 256 - 192]], axis=1)
 
-    def pack(t, u, half, k, own_turn):
+    def pack(u, half, k):
         to = partner(k)
-        first = target_domain(to // 4, lax.rem(to, 4), z, c, half) * 8
+        first = target_domain(to // 4, lax.rem(to, 4), z, c, half) * 192
         v = None
         for zz in range(8):
-            s = pltpu.roll(wide[u // 8, pl.ds(first + zz, 24, stride=128), :], 16 * zz, 1)
-            v = s if v is None else jnp.where(block24 == lax.rem(u + zz, 8), s, v)
-        return pltpu.roll(v, own_turn, 1)
+            s = planes[u // 8, pl.ds(pl.multiple_of(first + 24 * zz, 8), 24), :]
+            v = s if v is None else jnp.where(block24 == lax.rem(u + zz + dom // 2, 8), s, v)
+        return v
 
     def put(k, t, a, b):
         send1[k, t, 0] = a[:16].astype(BF16)
@@ -110,11 +115,10 @@
             send_sem=s1.at[part, slot], recv_sem=r1.at[part, source],
             device_id={"band": to, "dom": mirror}, device_id_type=MESH)
 
-    turn = (dom // 2) * 16
-    pl.semaphore_wait(barrier, 42)
+    pl.semaphore_wait(barrier, 26)
 
     def ends(k, _):
-        put(k, 0, *[pack(0, 12, half, k, turn + 8 * c) for half in range(2)])
+        put(k, 0, *[pltpu.roll(pack(12, half, k), 8 * c, 1) for half in range(2)])
         put(k, 1, r_left, r_right)
         copy1(k, band, 0, partner(k)).start()
         return 0
@@ -125,7 +129,7 @@
         part, k = i // 8 + 1, lax.rem(i, 8)
         for j in range(2):
             u = 2 * part - 2 + j
-            put(k, u + 2, *[pack(u + 2, u, half, k, turn) for half in range(2)])
+            put(k, u + 2, *[pack(u, half, k) for half in range(2)])
         copy1(k, band, part, partner(k)).start()
         return 0
 
@@ -312,7 +316,7 @@
                 pair.append(pltpu.roll(v, 128 - 16 * (s % 8), 1) if s % 8 else v)
             finish(12, zz, pair)
 
-    def step(order):
+    def step(order, g):
         a, b = 2 * order + 2, 22 - 2 * order
         now, other = (even, odd) if order % 2 == 0 else (odd, even)
         ring, following = rings[order % 2], rings[(order + 1) % 2]
@@ -348,7 +352,7 @@
                         if order < 3:
                             other[t, rows, :] = new
                         else:
-                            done[64 * t + 8 * (q - 8) : 64 * t + 8 * (q - 8) + 8, :] = new
+                            done[g, 64 * t + 8 * (q - 8) : 64 * t + 8 * (q - 8) + 8, :] = new
                         news.append(new)
                     if order < 3:
                         if q % 2:
@@ -358,7 +362,7 @@
                         pending = news
 
     def write(g):
-        return pltpu.make_async_copy(result.at[g], out_hbm.at[pl.ds(pl.multiple_of(64 * g, 64), 64)], lo.at[g])
+        return pltpu.make_async_copy(done.at[g], out_hbm.at[g], lo.at[g])
 
     arrive(0)
 
@@ -377,22 +381,7 @@
         for region, ref in enumerate((low, own, high)):
             unpack(region, ref, g)
         for order in range(4):
-            step(order)
-
-        def turn_out(o, _):
-            v = []
-            for t in range(25):
-                s = done[pl.ds(64 * t + o, 8, stride=8), :]
-                v.append(pltpu.roll(s, 16 * (t % 8), 1) if t % 8 else s)
-            rows = pl.ds(pl.multiple_of(8 * o, 8), 8)
-            for tau in range(25):
-                s = v[8 * tau % 25]
-                for beta in range(1, 8):
-                    s = jnp.where(block == beta, v[(8 * tau + beta) % 25], s)
-                result[g, rows, 128 * tau : 128 * tau + 128] = s
-            return 0
-
-        lax.fori_loop(0, 8, turn_out, 0)
+            step(order, g)
         write(g).start()
         return 0
 
@@ -420,6 +409,25 @@
     pl.when(has_low)(pot_copies[1].wait_send)
     for g in range(3):
         write(g).wait()
+
+
+def order_kernel(done, out_ref):
+    block = lax.broadcasted_iota(jnp.int32, (8, LANES), 1) // 16
+
+    def orbital(o, _):
+        v = []
+        for t in range(25):
+            s = done[0, pl.ds(64 * t + o, 8, stride=8), :]
+            v.append(pltpu.roll(s, 16 * (t % 8), 1) if t % 8 else s)
+        rows = pl.ds(pl.multiple_of(8 * o, 8), 8)
+        for tau in range(25):
+            s = v[8 * tau % 25]
+            for beta in range(1, 8):
+                s = jnp.where(block == beta, v[(8 * tau + beta) % 25], s)
+            out_ref[rows, 128 * tau : 128 * tau + 128] = s
+        return 0
+
+    lax.fori_loop(0, 8, orbital, 0)
 
 
 def y_weights():
@@ -441,31 +449,39 @@
     field = pltpu.VMEM((25, 192, LANES), F32)
     ring = pltpu.VMEM((5, 192, 1024), BF16)
     parts = pltpu.VMEM((8, 14, 3, 16, LANES), BF16)
-    out = pl.pallas_call(
+    done = pl.pallas_call(
         kernel,
-        out_shape=jax.ShapeDtypeStruct((192, NXY), F32),
+        out_shape=jax.ShapeDtypeStruct((3, 25 * 64, LANES), F32),
         in_specs=[anyspace, anyspace, anyspace, pl.BlockSpec(memory_space=pltpu.VMEM)],
         out_specs=anyspace,
         scratch_shapes=[
-            pltpu.VMEM((24, 128, 200), BF16),
+            pltpu.VMEM((24, 200, 128), BF16),
             pltpu.VMEM((24, 192), BF16),
             pltpu.VMEM((8, NXY), F32),
             pltpu.VMEM((2, 24 * 128, LANES), F32),
+            pltpu.VMEM((2, 128 * 24, LANES), F32),
             parts, parts,
             pltpu.VMEM((16, 3, 7, 16, LANES), BF16),
             pltpu.VMEM((2, 192, 256), BF16),
             group, group, group,
             plane, plane, plane,
             field, field, ring, ring, field,
-            pltpu.VMEM((25 * 64, LANES), F32),
-            pltpu.VMEM((3, 64, NXY), F32),
+            pltpu.VMEM((3, 25 * 64, LANES), F32),
             dma((7, 8)), dma((7, 8)), dma((3, 16)), dma((3, 16)),
             dma((2, 3)), dma((2, 3)), dma((2,)), dma((2,)), dma((3,)), dma((8,)), dma((3,)),
         ],
         compiler_params=pltpu.CompilerParams(
             collective_id=0, has_side_effects=True, vmem_limit_bytes=56 << 20),
         name="rotate_and_filter",
-    )(orbitals, rotation, potential, weights)
+    )(jnp.swapaxes(orbitals, 1, 2), rotation, potential, weights)
+    out = pl.pallas_call(
+        order_kernel,
+        grid=(3,),
+        out_shape=jax.ShapeDtypeStruct((192, NXY), F32),
+        in_specs=[pl.BlockSpec((1, 25 * 64, LANES), lambda g: (g, 0, 0))],
+        out_specs=pl.BlockSpec((64, NXY), lambda g: (g, 0)),
+        name="order",
+    )(done)
     return out.reshape(24, 8, NXY)
 
 

time: 86.6 us -> 77.9 us (0.90); the launches traced: 85.1 us -> 77.7 us
  local copies, waits for them, and re-layouts: 5.8 us -> 0 us
  Pallas kernels: 79.3 us -> 77.7 us
    unnamed x2 -> x0, local copies, waits for them, and re-layouts: 5.8 us -> none
    pallas_call x1 -> x2, Pallas kernels: 79.3 us -> 77.7 us  [the longest x1 72.7 us: body(): pl.pallas_call(kernel, out_shape=jax.ShapeDtypeStruct((3, 25 * 64, LANES)...]
where the time goes in v4:
time: 77.9 us; the launch traced here: 77.7 us
  Pallas kernels  77.7 us (100%)
    pallas_call x1, Pallas kernels, body(): pl.pallas_call(kernel, out_shape=jax.ShapeDtypeStruct((3, 25 * 64, LANES)...  72.7 us
    pallas_call x1, Pallas kernels, body(): pl.pallas_call(order_kernel, grid=(3,), out_shape=jax.ShapeDtypeStruct((1...  5.07 us

profile of v4, /device:TPU:97, one launch (start us, length us, event | category | flops | bytes accessed | tf_op | source)
XLA Modules:
  0.0 77.7 jit_solution(7528370215304732700)
XLA Ops:
  0.0 72.7 %rotate_and_filter.1.done = f32[3,1600,128]{2,1,0:T(8,128)} custom-call(bf16[24,200,128]{2,1,0:T(8,128)(2,1)} %bitcast.2, bf16[24,192]{1,0:T(8,128)(2,1)} %rot_hbm.1, f32[8,3200]{1,0:T(8,128)} %pot_hbm.1, bf16[512,256]{1,0:T(8,128)(2,1)} %constant.2.clone.wy_ref), custom_call_target="tpu_custom_call" | custom-call | tf_op jit(solution)/shard_map/rotate_and_filter/pallas_call | solution.py:452
  72.7 5.1 %order.1 = f32[192,3200]{1,0:T(8,128)} custom-call(f32[3,1600,128]{2,1,0:T(8,128)} %rotate_and_filter.1.done), custom_call_target="tpu_custom_call" | custom-call | tf_op jit(solution)/shard_map/order/pallas_call | solution.py:477
